TPU v7x, 32 devices: a whole 2x2x4 slice. The times are simulated.
32 devices in a mesh: prow: 4 (over z), pcol: 8 (over y, x, core).
Axes of the slice: x: 2, y: 2, z: 4, core: 2. Of those that a mesh axis runs over, the one named last changes fastest.
Arguments:
- ancestor_inv: float32 [16384, 16384], P('prow', 'pcol'), may hold values from -0.15625 to 0.15625
- l_scaled: float32 [2, 1536, 512], P(None, 'prow'), may hold values from -0.9 to 0.9
- diag_inv: float32 [2, 512, 512], replicated, may hold values from -6 to 6
- tile_lists: int32 [2, 6], replicated, may hold values from 0 to 63, as said below
Outputs:
- offdiag: float32 [2, 1536, 512], P(None, ('prow', 'pcol'))
- diag_block: float32 [2, 512, 512], replicated
Inputs may be any that keep to these rules, and one draw needn't show every extreme that they name: `tile_lists`: each row holds 6 different tile numbers; tile 0 and tile 64 - 1 are in every row.
All inputs are finite; a program needn't handle non-finite values.
Results may differ from a plain program's by a relative error of at most 0.0001.
Values sent between devices are 32-bit elements; how exact they have to be, the bound alone decides.
A program may use at most 192 MiB of HBM per device.

v0:
```python
import functools

import jax
import jax.numpy as jnp
from jax import lax
from jax.experimental import pallas as pl
from jax.experimental.pallas import tpu as pltpu
from jax.sharding import PartitionSpec as P

TILE = 256
W = 512
NS = 6
NSUP = 2
MESH = pl.DeviceIdType.MESH


def place(stage):
    row = lax.axis_index("prow")
    col = lax.axis_index("pcol")
    core = lax.rem(col, 2)
    chip = col // 2
    if stage == "row":
        return row, lambda m: (m, col)
    if stage == "chip":
        return chip, lambda m: (row, m * 2 + core)
    return core, lambda m: (row, chip * 2 + m)


def enter(peers):
    barrier = pltpu.get_barrier_semaphore()
    for peer in peers:
        pl.semaphore_signal(barrier, inc=1, device_id=peer, device_id_type=MESH)
    pl.semaphore_wait(barrier, len(peers))


def others(stage, size):
    me, device = place(stage)
    return [device(lax.rem(me + step, size)) for step in range(1, size)]


def send(src, dst, send_sem, recv_sem, peer):
    copy = pltpu.make_async_remote_copy(
        src_ref=src,
        dst_ref=dst,
        send_sem=send_sem,
        recv_sem=recv_sem,
        device_id=peer,
        device_id_type=MESH,
    )
    copy.start()
    return copy


def scatter_kernel(
    nrow, nchip, x_ref, y_ref, x_out, y_out, core_x, core_y, held, chip_in, sums, row_in, *sems
):
    core_send, core_recv, chip_send, chip_recv, row_send, row_recv = sems
    row, _ = place("row")
    chip, _ = place("chip")
    core, _ = place("core")
    rows, chips, cores = others("row", nrow), others("chip", nchip), others("core", 2)
    enter(rows + chips + cores)
    count = x_ref.shape[-2]
    pieces = [(step, sup) for step in [*range(1, nrow), 0] for sup in range(NSUP)]
    owners = [lax.rem(row + step, nrow) for step, _ in pieces]
    from_core = []
    for at, (_, sup) in enumerate(pieces):
        to = owners[at]
        from_core.append(
            [
                send(
                    src.at[sup, to, :, 1 - core],
                    dst.at[at],
                    core_send.at[at, which],
                    core_recv.at[at, which],
                    cores[0],
                )
                for which, (src, dst) in enumerate(((x_ref, core_x), (y_ref, core_y)))
            ]
        )
    from_chips = []
    from_rows = []

    def finish(at):
        step, sup = pieces[at]
        for copy in from_chips[at]:
            copy.wait_recv()
        total = held[at, chip]
        for near in range(nchip - 1):
            total += chip_in[at, near]
        sums[at] = total
        if step > 0:
            from_rows.append(
                send(
                    sums.at[at],
                    row_in.at[at],
                    row_send.at[at],
                    row_recv.at[at],
                    rows[step - 1],
                )
            )

    for at, (_, sup) in enumerate(pieces):
        for copy in from_core[at]:
            copy.wait_recv()
        held[at, :, :count] = x_ref[sup, owners[at], :, core] + core_x[at]
        held[at, :, count:] = y_ref[sup, owners[at], :, core] + core_y[at]
        from_chips.append(
            [
                send(
                    held.at[at, lax.rem(chip + near + 1, nchip)],
                    chip_in.at[at, near],
                    chip_send.at[at, near],
                    chip_recv.at[at, near],
                    peer,
                )
                for near, peer in enumerate(chips)
            ]
        )
        if at >= 2:
            finish(at - 2)
    finish(len(pieces) - 2)
    finish(len(pieces) - 1)
    for copy in from_rows:
        copy.wait_recv()
    for sup in range(NSUP):
        total = sums[(nrow - 1) * NSUP + sup]
        for step in range(nrow - 1):
            total += row_in[step * NSUP + sup]
        x_out[sup] = total[:count]
        y_out[sup] = total[count:]
    for group in from_core + from_chips + [from_rows]:
        for copy in group:
            copy.wait_send()


def scatter(x, y, nrow, nchip, collective_id):
    count, part = x.shape[-2], y.shape[-2]
    n = nrow * NSUP
    f32 = jnp.float32
    vmem = pl.BlockSpec(memory_space=pltpu.VMEM)
    core, chip, row = (n, 2), (n, nchip - 1), (n - NSUP,)
    return pl.pallas_call(
        functools.partial(scatter_kernel, nrow, nchip),
        out_shape=[
            jax.ShapeDtypeStruct((NSUP, count, W), f32),
            jax.ShapeDtypeStruct((NSUP, part, W), f32),
        ],
        in_specs=[vmem, vmem],
        out_specs=[vmem, vmem],
        scratch_shapes=[
            pltpu.VMEM((n, nchip, count, W), f32),
            pltpu.VMEM((n, nchip, part, W), f32),
            pltpu.VMEM((n, nchip, count + part, W), f32),
            pltpu.VMEM((n, nchip - 1, count + part, W), f32),
            pltpu.VMEM((n, count + part, W), f32),
            pltpu.VMEM((n - NSUP, count + part, W), f32),
            *(pltpu.SemaphoreType.DMA(s) for s in (core, core, chip, chip, row, row)),
        ],
        compiler_params=pltpu.CompilerParams(
            collective_id=collective_id,
            has_side_effects=True,
            vmem_limit_bytes=44 * 1024 * 1024,
        ),
    )(x, y)


def gather_kernel(nrow, nchip, known, x_ref, out_ref, *sems):
    row_send, row_recv, chip_send, chip_recv, core_send, core_recv = sems
    row, _ = place("row")
    chip, _ = place("chip")
    core, _ = place("core")
    rows, chips, cores = others("row", nrow), others("chip", nchip), others("core", 2)
    enter(rows + chips + cores)
    started = []

    def forward(*args):
        started.append(send(*args))
        return started[-1]

    mine = out_ref.at[:, row, chip, core]
    from_rows = [
        forward(x_ref, mine, row_send.at[step], row_recv.at[step], peer)
        for step, peer in enumerate(rows)
    ]
    from_chips = []
    last = []
    for near in range(1 if known else 0, nrow):
        src = x_ref
        slot = mine
        if near > 0:
            from_rows[near - 1].wait_recv()
            slot = out_ref.at[:, lax.rem(row - near + nrow, nrow), chip, core]
            src = slot
        for step, peer in enumerate(chips):
            from_chips.append(
                (
                    near,
                    step + 1,
                    forward(src, slot, chip_send.at[step, near], chip_recv.at[step, near], peer),
                )
            )
        last.append(forward(src, slot, core_send.at[0, near], core_recv.at[0, near], cores[0]))
    for near, step, copy in from_chips:
        copy.wait_recv()
        slot = out_ref.at[
            :, lax.rem(row - near + nrow, nrow), lax.rem(chip - step + nchip, nchip), core
        ]
        last.append(
            forward(slot, slot, core_send.at[step, near], core_recv.at[step, near], cores[0])
        )
    for copy in last:
        copy.wait_recv()
    for copy in started:
        copy.wait_send()


def gather(x, nrow, nchip, collective_id, plane=None):
    shape = (x.shape[0], nrow, nchip, 2) + x.shape[1:]
    row, chip, core = ((nrow - 1,), (nchip - 1, nrow), (nchip, nrow))
    full = pl.pallas_call(
        functools.partial(gather_kernel, nrow, nchip, plane is not None),
        out_shape=jax.ShapeDtypeStruct(shape, x.dtype),
        in_specs=[pl.BlockSpec(memory_space=pl.ANY)],
        out_specs=pl.BlockSpec(memory_space=pl.ANY),
        scratch_shapes=[
            pltpu.SemaphoreType.DMA(n) for n in (row, row, chip, chip, core, core)
        ],
        compiler_params=pltpu.CompilerParams(
            collective_id=collective_id, has_side_effects=True
        ),
    )(x)
    if plane is not None:
        plane = plane.reshape(x.shape[0], 1, nchip, 2, *x.shape[1:])
        return lax.dynamic_update_slice(full, plane, (0, place("row")[0], 0, 0, 0, 0))
    where = (0, place("row")[0], place("chip")[0], place("core")[0], 0, 0)
    return lax.dynamic_update_slice(full, x[:, None, None, None], where)


def dot(a, b, contract):
    def split(x):
        high = x.astype(jnp.bfloat16)
        return high, (x - high.astype(jnp.float32)).astype(jnp.bfloat16)

    def one(x, y):
        return lax.dot_general(
            x, y, ((contract, (0,)), ((), ())), preferred_element_type=jnp.float32
        )

    a_high, a_low = split(a)
    b_high, b_low = split(b)
    return one(a_low, b_high) + one(a_high, b_low) + one(a_high, b_high)


def product_kernel(rows_ref, cols_ref, *refs):
    *tiles, l_ref, p_ref, d_ref = refs
    sup, i = pl.program_id(0), pl.program_id(1)
    row_hit = rows_ref[sup, i] >= 0

    @pl.when(i == 0)
    def _():
        d_ref[...] = jnp.zeros_like(d_ref)

    p_ref[...] = jnp.zeros_like(p_ref)

    @pl.when(row_hit)
    def _():
        for j, a_ref in enumerate(tiles):

            @pl.when(cols_ref[sup, j] >= 0)
            def _():
                p_ref[0] -= dot(a_ref[...], l_ref[0, j * TILE:(j + 1) * TILE, :], (1,))

        block = l_ref[0, pl.ds(pl.multiple_of(i * TILE, TILE), TILE), :]
        d_ref[0] += dot(block, p_ref[0], (0,))


def products(rows, cols, ancestor, lfull):
    def tile(j):
        def index(sup, i, rows_ref, cols_ref):
            row, col = rows_ref[sup, i], cols_ref[sup, j]
            hit = (row >= 0) & (col >= 0)
            return jnp.where(hit, row, 0), jnp.where(hit, col, 0)

        return pl.BlockSpec((TILE, TILE), index)

    total = lfull.shape[1]
    return pl.pallas_call(
        product_kernel,
        out_shape=(
            jax.ShapeDtypeStruct((NSUP, total, W), jnp.float32),
            jax.ShapeDtypeStruct((NSUP, W, W), jnp.float32),
        ),
        grid_spec=pltpu.PrefetchScalarGridSpec(
            num_scalar_prefetch=2,
            grid=(NSUP, NS),
            in_specs=[tile(j) for j in range(NS)]
            + [pl.BlockSpec((1, total, W), lambda sup, i, *_: (sup, 0, 0))],
            out_specs=[
                pl.BlockSpec((1, TILE, W), lambda sup, i, *_: (sup, i, 0)),
                pl.BlockSpec((1, W, W), lambda sup, i, *_: (sup, 0, 0)),
            ],
        ),
        compiler_params=pltpu.CompilerParams(vmem_limit_bytes=40 * 1024 * 1024),
    )(rows, cols, *[ancestor] * NS, lfull)


ROW_TILES = 16
COL_TILES = 8
UNIT = 16
ORDER = (3, 1, 2, 0)


def flip(value, bit):
    return value + bit - 2 * bit * lax.rem(lax.div(value, bit), 2)


def split(x):
    high = x.astype(jnp.bfloat16)
    return high, (x - high.astype(jnp.float32)).astype(jnp.bfloat16)


def dot3(a, b, contract):
    def one(x, y):
        return lax.dot_general(
            x, y, ((contract, (0,)), ((), ())), preferred_element_type=jnp.float32
        )

    (a_high, a_low), (b_high, b_low) = a, b
    return one(a_low, b_high) + one(a_high, b_low) + one(a_high, b_high)


def fused_kernel(rcap, ccap, *refs):
    t_ref, a_ref, l_ref, d_ref, off_ref, diag_ref, a_buf, b_high, b_low, tab, dinv = refs[:11]
    local_sem, send_sem, recv_sem, z_send, z_recv = refs[-5:]
    per_sup = refs[11:-5]
    groups = [per_sup[i * NSUP:(i + 1) * NSUP] for i in range(len(per_sup) // NSUP)]
    l_buf, p_buf, core_in, held, chip_in, mid_buf, total, d_buf, d_core, d_sum, d_in, e_buf, e_in, f_buf = groups
    row = lax.axis_index("prow")
    col = lax.axis_index("pcol")
    core = lax.rem(col, 2)
    chip = lax.div(col, 2)
    rows = [row, flip(row, 1), flip(row, 2), flip(flip(row, 1), 2)]
    chips = [chip, flip(chip, 1), flip(chip, 2), flip(flip(chip, 1), 2)]
    sibling = (row, chip * 2 + 1 - core)

    def on_row(s):
        return rows[s], col

    def on_chip(d):
        return row, chips[d] * 2 + core

    def across(d):
        return row, chips[d] * 2 + 1 - core

    used = {}

    def send(src, dst, peer, group, shared=None):
        at = used.setdefault(shared or len(used), len(used))
        copy = pltpu.make_async_remote_copy(
            src_ref=src,
            dst_ref=dst,
            send_sem=send_sem.at[group],
            recv_sem=recv_sem.at[at],
            device_id=peer,
            device_id_type=MESH,
        )
        copy.start()
        return copy

    def gathered(shared, ref, group=0):
        return pltpu.make_async_remote_copy(
            src_ref=ref,
            dst_ref=ref,
            send_sem=send_sem.at[group],
            recv_sem=recv_sem.at[used[shared]],
            device_id=sibling,
            device_id_type=MESH,
        )

    local = []

    def fetch(src, dst):
        copy = pltpu.make_async_copy(src, dst, local_sem.at[len(local)])
        copy.start()
        local.append(copy)
        return copy

    quarter = l_ref.shape[1]
    half = quarter // 2
    own_l = [
        [
            fetch(l_ref.at[sup, :, :, :, w * 128:(w + 1) * 128],
                  l_buf[sup].at[w, pl.ds(row * quarter, quarter)])
            for w in range(4)
        ]
        for sup in range(NSUP)
    ]
    own_a = [
        fetch(a_ref.at[:, :, j * TILE:(j + 1) * TILE], a_buf.at[j]) for j in range(COL_TILES)
    ]
    d_rows = 256 * core + 64 * row
    lanes = pl.ds(pl.multiple_of(chip * 128, 128), 128)
    own_d = fetch(d_ref.at[:, pl.ds(pl.multiple_of(d_rows, 64), 64), lanes], dinv)

    peers = [on_row(s) for s in (1, 2, 3)] + [on_chip(d) for d in (1, 2, 3)]
    peers += [sibling] + [across(d) for d in (1, 2, 3)]
    enter(peers)

    middle = lax.div(row * (3 - row), 2)
    sources = [
        rows[1],
        rows[2] + middle * (rows[3] - rows[2]),
        rows[3] + middle * (rows[2] - rows[3]),
    ]

    def piece(sup, source, d, begin=0, size=None):
        size = half if size is None else size
        return l_buf[sup].at[chips[d], pl.ds(source * quarter + core * half + begin, size)]

    def z_copy(sup, slot, src, dst, which, s):
        return pltpu.make_async_remote_copy(
            src_ref=src,
            dst_ref=dst,
            send_sem=z_send.at[sup, which],
            recv_sem=z_recv.at[sup, slot],
            device_id=on_row(s),
            device_id_type=MESH,
        )

    def z_own(sup, slot, which, s):
        return z_copy(
            sup, slot, l_ref.at[sup, pl.ds(core * half, half), :, :, lanes],
            piece(sup, row, 0), which, s)

    def z_pass(sup, slot, which):
        block = piece(sup, sources[slot], 0)
        return z_copy(sup, slot, block, block, which, 1)

    def send_rows(sup):
        z_own(sup, 0, 0, 1).start()

        @pl.when(middle == 1)
        def _():
            z_own(sup, 1, 1, 3).start()

        @pl.when(middle == 0)
        def _():
            z_own(sup, 2, 1, 2).start()

    from_x, from_y, from_far = ([[] for _ in range(NSUP)] for _ in range(3))

    def spread_row(sup, slot):
        z_own(sup, slot, 0, 1).wait_recv()
        if slot > 0:
            @pl.when(middle == 1)
            def _():
                z_pass(sup, slot, slot + 1).start()

        block = piece(sup, sources[slot], 0)
        from_x[sup].append(send(block, block, on_chip(1), sup))
        from_y[sup].append(send(block, block, on_chip(2), sup))
        send(block, block, sibling, sup, ("l", sup))

    def spread_chips(sup):
        part = half // 2
        for slot, source in enumerate(sources):
            from_x[sup][slot].wait_recv()
            block = piece(sup, source, 1, 0, part)
            from_far[sup].append((source, 0, send(block, block, on_chip(2), sup)))
            from_y[sup][slot].wait_recv()
            block = piece(sup, source, 2, part, part)
            from_far[sup].append((source, part, send(block, block, on_chip(1), sup)))
            for d in (1, 2):
                block = piece(sup, source, d)
                send(block, block, sibling, sup, ("l", sup))

    def finish_l(sup):
        part = half // 2
        for source, begin, copy in from_far[sup]:
            copy.wait_recv()
            block = piece(sup, source, 3, begin, part)
            send(block, block, sibling, sup, ("l", sup))
        gathered(("l", sup), l_buf[sup].at[:, :3 * half]).wait_recv()
        for copy in own_l[sup]:
            copy.wait()

    def finish_rows(sup):
        z_own(sup, 0, 0, 1).wait_send()
        z_own(sup, 1, 1, 1).wait_send()

        @pl.when(middle == 1)
        def _():
            for slot in (1, 2):
                z_pass(sup, slot, slot + 1).wait_send()

    width = 2 * rcap + 2 * NS + 3 * ccap

    def make_table(sup):
        tiles = [t_ref[sup, k] for k in range(NS)]

        def ranked(base, extent, cap):
            seen = jnp.int32(0)
            found = []
            for k in range(NS):
                at = tiles[k] - base
                hit = ((at >= 0) & (at < extent)).astype(jnp.int32)
                found.append((at, hit, seen))
                seen = seen + hit
            slots = []
            for s in range(cap):
                tile, pos, valid = jnp.int32(0), jnp.int32(0), jnp.int32(0)
                for k, (at, hit, rank) in enumerate(found):
                    here = hit * (rank == s).astype(jnp.int32)
                    tile = tile + here * at
                    pos = pos + here * k
                    valid = valid + here
                slots.append((tile, pos, valid))
            return slots, found

        slots, found = ranked(row * ROW_TILES, ROW_TILES, rcap)
        base = sup * width
        for s, (tile, pos, valid) in enumerate(slots):
            tab[base + s] = tile + (valid - 1) * ROW_TILES
            tab[base + rcap + s] = pos
        base += 2 * rcap
        for k, (_, hit, rank) in enumerate(found):
            tab[base + k] = hit
            tab[base + NS + k] = jnp.minimum(rank, rcap - 1)
        base += 2 * NS
        slots, _ = ranked(col * COL_TILES, COL_TILES, ccap)
        for s, (tile, pos, valid) in enumerate(slots):
            tab[base + s] = tile
            tab[base + ccap + s] = pos
            tab[base + 2 * ccap + s] = valid

    from_core = [[] for _ in range(NSUP)]

    def product(sup):
        base = sup * width
        cols = base + 2 * rcap + 2 * NS
        for t in range(ccap):
            pos = tab[cols + ccap + t]
            for w in range(4):
                block = l_buf[sup][w, pl.ds(pos * UNIT, UNIT)].reshape(TILE, 128)
                high, low = split(block)
                b_high[t * TILE:(t + 1) * TILE, w * 128:(w + 1) * 128] = high
                b_low[t * TILE:(t + 1) * TILE, w * 128:(w + 1) * 128] = low

        @pl.loop(0, rcap)
        def _(s):
            at = tab[base + s]
            tiles = []
            for t in range(ccap):
                hit = (at >= 0) & (tab[cols + 2 * ccap + t] > 0)
                block = a_buf[tab[cols + t], jnp.maximum(at, 0)]
                tiles.append(jnp.where(hit, block, 0.0))
            a = split(jnp.concatenate(tiles, axis=1))
            result = dot3(a, (b_high[...], b_low[...]), (1,))
            for w in range(4):
                block = result[:, w * 128:(w + 1) * 128].reshape(UNIT, 2, 8, 128)
                p_buf[sup][0, w, s] = block[:, 0]
                p_buf[sup][1, w, s] = block[:, 1]

        for d in ORDER:
            from_core[sup].append(
                send(p_buf[sup].at[1 - core, chips[d]], core_in[sup].at[chips[d]], sibling, NSUP + sup)
            )

    from_chips = [[] for _ in range(NSUP)]

    parts = (slice(0, UNIT // 2), slice(UNIT // 2, UNIT))

    def reduce_send(sup):
        for at, d in enumerate(ORDER):
            from_core[sup][at].wait_recv()
            w = chips[d]
            held[sup][w] = p_buf[sup][core, w] + core_in[sup][w]
            for which, near in enumerate((1, 2)):
                if d in (near, 3):
                    src = held[sup].at[w, :, parts[which]]
                    to = chip_in[sup].at[2 * which + (d == 3)]
                    from_chips[sup].append((2 * which + (d == 3), send(src, to, on_chip(near), NSUP + sup)))

    def reduce_pass(sup):
        first = dict(from_chips[sup])
        for which, near in enumerate((1, 2)):
            first[2 * which + 1].wait_recv()
            other = 3 - near
            block = held[sup][chips[other], :, parts[which]]
            mid_buf[sup][which] = block + chip_in[sup][2 * which + 1]
            from_chips[sup].append(
                (
                    4 + which,
                    send(mid_buf[sup].at[which], chip_in[sup].at[4 + which], on_chip(other), NSUP + sup),
                )
            )

    from_d = [None] * NSUP

    def reduce_finish(sup):
        for at, copy in from_chips[sup]:
            if at in (0, 2, 4, 5):
                copy.wait_recv()
        for which in range(2):
            block = held[sup][chip, :, parts[which]] + chip_in[sup][2 * which]
            total[sup][:, parts[which]] = block + chip_in[sup][4 + which]
        base = sup * width
        picked = []
        for s in range(rcap):
            pos = tab[base + rcap + s]
            picked.append(
                jnp.concatenate(
                    [
                        l_buf[sup][w, pl.ds(pos * UNIT, UNIT), core].reshape(128, 128)
                        for w in range(4)
                    ],
                    axis=1,
                )
            )
        left = split(jnp.concatenate(picked, axis=0))
        right = split(total[sup][...].reshape(rcap * 128, 128))
        d_buf[sup][...] = dot3(left, right, (0,)).reshape(2, 256, 128)
        from_d[sup] = send(d_buf[sup].at[1 - core], d_core[sup], sibling, 2 * NSUP)

    def listed(sup, to, put):
        base = sup * width + 2 * rcap
        for j in range(3):
            unit = 3 * to + j
            k = lax.div(unit, 2)
            begin = pl.multiple_of(8 * lax.rem(unit, 2), 8)
            block = total[sup][tab[base + NS + k], pl.ds(begin, 8)]
            put(j, jnp.where(tab[base + k] > 0, block, 0.0))

    def exchange(sup):
        for s in (1, 2, 3):
            def put(j, block):
                e_buf[sup][s - 1, 8 * j:8 * j + 8] = block

            listed(sup, rows[s], put)
            send(e_buf[sup].at[s - 1], e_in[sup].at[s - 1], on_row(s), 2 * NSUP + 1, ("e", sup))

    def diag_rows(sup):
        from_d[sup].wait_recv()
        d_sum[sup][...] = (d_buf[sup][core] + d_core[sup][...]).reshape(4, 64, 128)
        for s in (1, 2, 3):
            send(d_sum[sup].at[rows[s]], d_in[sup].at[s - 1], on_row(s), 2 * NSUP, ("d", sup))

    def diag_piece(sup):
        gathered(("d", sup), d_in[sup]).wait_recv()
        mine = diag_ref.at[sup, pl.ds(pl.multiple_of(d_rows, 64), 64), lanes]
        value = d_sum[sup][row] + d_in[sup][0] + d_in[sup][1] + d_in[sup][2]
        mine[...] = dinv[sup] + value
        for s in (1, 2, 3):
            send(mine, mine, on_row(s), 2 * NSUP, ("g", sup))

    from_gc = [[] for _ in range(NSUP)]

    def diag_block(sup, d):
        at = pl.ds(pl.multiple_of(chips[d] * 128, 128), 128)
        return diag_ref.at[sup, pl.ds(pl.multiple_of(256 * core, 256), 256), at]

    def diag_chips(sup):
        gathered(("g", sup), d_in[sup]).wait_recv()
        block = diag_block(sup, 0)
        for d in (1, 2, 3):
            from_gc[sup].append(send(block, block, on_chip(d), 2 * NSUP))
        send(block, block, sibling, 2 * NSUP, "gs")

    def diag_cores(sup):
        for d in (1, 2, 3):
            from_gc[sup][d - 1].wait_recv()
            block = diag_block(sup, d)
            send(block, block, sibling, 2 * NSUP, "gs")

    def owners(sup):
        gathered(("e", sup), e_in[sup]).wait_recv()

        def put(j, block):
            at = slice(8 * j, 8 * j + 8)
            rest = e_in[sup][0, at] + e_in[sup][1, at] + e_in[sup][2, at]
            f_buf[sup][at] = -(block + rest)

        listed(sup, row, put)
        place_at = off_ref.at[sup, :, core, :, lanes]

        def share(to):
            return f_buf[sup].at[pl.ds(3 * to, 3)]

        for d in (1, 2, 3):
            for peer in (on_chip(d), across(d)):
                send(share(peer[1]), place_at, peer, 2 * NSUP + 1, "o")
        send(share(sibling[1]), place_at, sibling, 2 * NSUP + 1, "o")
        off_ref[sup, :, core, :, lanes] = f_buf[sup][pl.ds(3 * col, 3)]

    send_rows(0)
    for sup in range(NSUP):
        make_table(sup)
    spread_row(0, 0)
    send_rows(1)
    spread_row(0, 1)
    spread_row(0, 2)
    spread_chips(0)
    for slot in range(3):
        spread_row(1, slot)
    finish_l(0)
    for copy in own_a:
        copy.wait()
    product(0)
    spread_chips(1)
    reduce_send(0)
    finish_l(1)
    product(1)
    reduce_pass(0)
    reduce_send(1)
    reduce_finish(0)
    reduce_pass(1)
    diag_rows(0)
    exchange(0)
    reduce_finish(1)
    own_d.wait()
    diag_piece(0)
    diag_rows(1)
    exchange(1)
    diag_chips(0)
    diag_piece(1)
    owners(0)
    diag_chips(1)
    diag_cores(0)
    owners(1)
    diag_cores(1)
    for sup in range(NSUP):
        finish_rows(sup)
    gathered("gs", l_buf[0].at[:, :32]).wait_recv()
    gathered("o", l_buf[0].at[0, :21]).wait_recv()
    for sup in range(NSUP):
        gathered("o", l_buf[sup].at[:, :63], sup).wait_send()
        gathered("o", p_buf[sup].at[:, :, :, :14], NSUP + sup).wait_send()
    gathered("o", l_buf[0].at[:, :76], 2 * NSUP).wait_send()
    gathered("o", l_buf[0].at[0, :93], 2 * NSUP + 1).wait_send()


def fused(rcap, ccap, tile_lists, ancestor, l_scaled, diag_inv):
    f32 = jnp.float32
    total_rows = l_scaled.shape[1] * 4
    units = total_rows // UNIT
    view = l_scaled.reshape(NSUP, l_scaled.shape[1] // UNIT, 2, 8, W)
    any_space = pl.BlockSpec(memory_space=pl.ANY)
    vmem = pl.BlockSpec(memory_space=pltpu.VMEM)
    block = (rcap, UNIT, 8, 128)
    per_sup = [
        (4, units, 2, 8, 128),
        (2, 4) + block,
        (4,) + block,
        (4,) + block,
        (6, rcap, UNIT // 2, 8, 128),
        (2, rcap, UNIT // 2, 8, 128),
        block,
        (2, 256, 128),
        (256, 128),
        (4, 64, 128),
        (3, 64, 128),
        (3, 24, 8, 128),
        (3, 24, 8, 128),
        (24, 8, 128),
    ]
    scratch = [
        pltpu.VMEM((COL_TILES, ROW_TILES, TILE, TILE), f32),
        pltpu.VMEM((ccap * TILE, W), jnp.bfloat16),
        pltpu.VMEM((ccap * TILE, W), jnp.bfloat16),
        pltpu.SMEM((NSUP * (2 * rcap + 2 * NS + 3 * ccap),), jnp.int32),
        pltpu.VMEM((NSUP, 64, 128), f32),
    ]
    for shape in per_sup:
        scratch += [pltpu.VMEM(shape, f32)] * NSUP
    scratch += [
        pltpu.SemaphoreType.DMA((4 * NSUP + COL_TILES + 1,)),
        pltpu.SemaphoreType.DMA((2 * NSUP + 2,)),
        pltpu.SemaphoreType.DMA((NSUP * (6 + 6 + 1 + 4 + 6 + 1 + 1 + 1 + 1 + 3) + 2,)),
        pltpu.SemaphoreType.DMA((NSUP, 4)),
        pltpu.SemaphoreType.DMA((NSUP, 3)),
    ]
    off, diag = pl.pallas_call(
        functools.partial(fused_kernel, rcap, ccap),
        out_shape=[
            jax.ShapeDtypeStruct((NSUP, 3, 2, 8, W), f32),
            jax.ShapeDtypeStruct((NSUP, W, W), f32),
        ],
        in_specs=[pl.BlockSpec(memory_space=pltpu.SMEM), any_space, any_space, any_space],
        out_specs=[vmem, vmem],
        scratch_shapes=scratch,
        compiler_params=pltpu.CompilerParams(
            collective_id=6 + rcap,
            has_side_effects=True,
            vmem_limit_bytes=60 * 1024 * 1024,
        ),
    )(tile_lists, ancestor.reshape(ROW_TILES, TILE, -1), view, diag_inv)
    return off.reshape(NSUP, 48, W), diag


FOURS = 0x44444444


def packed_counts(tile_lists):
    field = 4 * jnp.arange(NSUP, dtype=jnp.int32)[:, None] + tile_lists // ROW_TILES
    return jnp.sum(jnp.left_shift(jnp.int32(1), 4 * field))


def per_device(nrow, ncol, ancestor_inv, l_scaled, diag_inv, tile_lists):
    if (nrow, ncol) == (4, 8):
        args = (tile_lists, ancestor_inv, l_scaled, diag_inv)
        counts = packed_counts(tile_lists)
        low, middle, top = (functools.partial(fused, cap, cap) for cap in (3, 4, NS - 1))

        def more(*rest):
            fives = counts & jnp.left_shift(counts, 2) & FOURS
            return lax.cond(fives == 0, middle, top, *rest)

        return lax.cond(counts & FOURS == 0, low, more, *args)
    return stepwise(nrow, ncol, ancestor_inv, l_scaled, diag_inv, tile_lists)


def stepwise(nrow, ncol, ancestor_inv, l_scaled, diag_inv, tile_lists):
    nchip = ncol // 2
    tile_rows = ancestor_inv.shape[0] // TILE
    tile_cols = ancestor_inv.shape[1] // TILE
    row_pos = lax.axis_index("prow")
    col_pos = lax.axis_index("pcol")
    count = l_scaled.shape[1] // ncol
    part = W // (nrow * ncol)
    total = l_scaled.shape[1] * nrow

    share = lax.dynamic_slice_in_dim(l_scaled, col_pos * count, count, 1)
    lfull = gather(share, nrow, nchip, 1, l_scaled).reshape(NSUP, total, W)

    rows = tile_lists - row_pos * tile_rows
    rows = jnp.where((rows >= 0) & (rows < tile_rows), rows, -1)
    cols = tile_lists - col_pos * tile_cols
    cols = jnp.where((cols >= 0) & (cols < tile_cols), cols, -1)
    rows = jnp.where(jnp.max(cols, axis=1, keepdims=True) >= 0, rows, -1)
    partial, terms = products(rows, cols, ancestor_inv, lfull)

    mine, term = scatter(
        partial.reshape(NSUP, nrow, nchip, 2, count, W),
        terms.reshape(NSUP, nrow, nchip, 2, part, W),
        nrow,
        nchip,
        2,
    )
    diag = gather(term, nrow, nchip, 5).reshape(NSUP, W, W)
    return mine, diag_inv - diag


def solution(mesh):
    placed = (P("prow", "pcol"), P(None, "prow", None), P(), P())
    return jax.shard_map(
        functools.partial(per_device, mesh.shape["prow"], mesh.shape["pcol"]),
        mesh=mesh,
        in_specs=placed,
        out_specs=(P(None, ("prow", "pcol"), None), P()),
        check_vma=False,
    )
```

profile of v0, /device:TPU:0, one launch (start us, length us, event | category | flops | bytes accessed | tf_op | source)
XLA Modules:
  0.0 85.5 jit_solution(16913625847963339843)
XLA Ops:
  0.6 1.4 %shift-left_reduce_fusion = s32[]{:T(128)} fusion(s32[2,6]{1,0:T(2,128)} %param.11, s32[2]{0:T(128)S(1)} %iota_multiply_fusion), kind=kLoop, calls=%fused_computation.4 | loop fusion | flops 227 | bytes 60 | tf_op jit(solution)/shard_map/reduce_sum | solution.py:806
  2.7 80.9 %conditional.2 = ((f32[2,48,512]{2,1,0:T(8,128)S(1)}, f32[2,512,512]{2,1,0:T(8,128)S(1)})) conditional(s32[]{:T(128)} %convert_element_type.6, (s32[]{:T(128)}, f32[4096,2048]{1,0:T(8,128)}, f32[2,384,512]{2,1,0:T(8,128)}, s32[2,6]{1,0:T(2,128)}, f32[2,512,512]{2,1,0:T(8,128)}) %tuple.22, (f32[4096,2048]{1,0:T(8,128)}, f32[2,384,512]{2,1,0:T(8,128)}, ...), branch_computations={%region_1.4_spmd, %region_4.5_spmd} | conditional | flops 5 | bytes 106 | solution.py:819
  2.9 80.7 %branch_1_fun.3 = (f32[2,3,2,8,512]{4,3,2,1,0:T(8,128)S(1)}, f32[2,512,512]{2,1,0:T(8,128)S(1)}) custom-call(s32[2,6]{1,0:T(2,128)} %get-tuple-element.51.refs_0_, f32[16,256,2048]{2,1,0:T(8,128)} %bitcast.11, f32[2,24,2,8,512]{4,3,2,1,0:T(8,128)} %bitcast.14, f32[2,512,512]{2,1,0:T(8,128)} %get-tuple-element.54.refs_3_), custom_call_target="tpu_custom_call" | custom-call | tf_op jit(solution)/shard_map/cond/branch_1_fun/pallas_call | solution.py:783
  83.5 0.7 copy.20
  84.2 1.3 %copy.21 = f32[2,512,512]{2,1,0:T(8,128)} copy(f32[2,512,512]{2,1,0:T(8,128)S(1)} %get-tuple-element.74) | data formatting | bytes 4194304
  (1 shorter events, 0.0 us)
where the time goes:
time: 85.7 us; the launch traced here: 85.5 us
  Pallas kernels  80.7 us (94%)
  local copies, waits for them, and re-layouts  2 us (2%)
  other arithmetic  1.39 us (2%)
  between operations  1.3 us (2%)
    pallas_call x1, Pallas kernels, fused(): pl.pallas_call(functools.partial(fused_kernel, rcap, ccap), out_shape=[ja...  80.7 us
    unnamed x2, local copies, waits for them, and re-layouts  2 us

commit v1 on v0

--- a/solution.py
+++ b/solution.py
@@ -652,25 +652,30 @@
         value = d_sum[sup][row] + d_in[sup][0] + d_in[sup][1] + d_in[sup][2]
         mine[...] = dinv[sup] + value
         for s in (1, 2, 3):
-            send(mine, mine, on_row(s), 2 * NSUP, ("g", sup))
-
-    from_gc = [[] for _ in range(NSUP)]
+            from_g[sup].append(send(mine, mine, on_row(s), 2 * NSUP))
+        for d in (1, 2, 3):
+            send(mine, mine, on_chip(d), 2 * NSUP, ("c", sup, d))
+
+    from_g = [[] for _ in range(NSUP)]
 
     def diag_block(sup, d):
         at = pl.ds(pl.multiple_of(chips[d] * 128, 128), 128)
         return diag_ref.at[sup, pl.ds(pl.multiple_of(256 * core, 256), 256), at]
 
     def diag_chips(sup):
-        gathered(("g", sup), d_in[sup]).wait_recv()
+        for s in (1, 2, 3):
+            from_g[sup][s - 1].wait_recv()
+            at = pl.ds(pl.multiple_of(256 * core + 64 * rows[s], 64), 64)
+            block = diag_ref.at[sup, at, lanes]
+            for d in (1, 2, 3):
+                send(block, block, on_chip(d), 2 * NSUP, ("c", sup, d))
         block = diag_block(sup, 0)
-        for d in (1, 2, 3):
-            from_gc[sup].append(send(block, block, on_chip(d), 2 * NSUP))
         send(block, block, sibling, 2 * NSUP, "gs")
 
     def diag_cores(sup):
         for d in (1, 2, 3):
-            from_gc[sup][d - 1].wait_recv()
             block = diag_block(sup, d)
+            gathered(("c", sup, d), block).wait_recv()
             send(block, block, sibling, 2 * NSUP, "gs")
 
     def owners(sup):
@@ -714,19 +719,19 @@
     reduce_pass(0)
     reduce_send(1)
     reduce_finish(0)
+    exchange(0)
     reduce_pass(1)
     diag_rows(0)
-    exchange(0)
     reduce_finish(1)
+    diag_rows(1)
     own_d.wait()
     diag_piece(0)
-    diag_rows(1)
+    diag_chips(0)
+    owners(0)
+    diag_piece(1)
     exchange(1)
-    diag_chips(0)
-    diag_piece(1)
-    owners(0)
+    diag_cores(0)
     diag_chips(1)
-    diag_cores(0)
     owners(1)
     diag_cores(1)
     for sup in range(NSUP):
@@ -776,7 +781,7 @@
     scratch += [
         pltpu.SemaphoreType.DMA((4 * NSUP + COL_TILES + 1,)),
         pltpu.SemaphoreType.DMA((2 * NSUP + 2,)),
-        pltpu.SemaphoreType.DMA((NSUP * (6 + 6 + 1 + 4 + 6 + 1 + 1 + 1 + 1 + 3) + 2,)),
+        pltpu.SemaphoreType.DMA((NSUP * (6 + 6 + 1 + 4 + 6 + 1 + 1 + 3 + 3 + 1) + 2,)),
         pltpu.SemaphoreType.DMA((NSUP, 4)),
         pltpu.SemaphoreType.DMA((NSUP, 3)),
     ]

time: 85.7 us -> 79 us (0.922)
  Pallas kernels: 80.7 us -> 74 us
    pallas_call x1, Pallas kernels: 80.7 us -> 74 us  [fused(): pl.pallas_call(functools.partial(fused_kernel, rcap, ccap), out_shape=[ja...]
where the time goes in v1:
time: 79 us; the launch traced here: 78.9 us
  Pallas kernels  74 us (94%)
  local copies, waits for them, and re-layouts  2 us (3%)
  other arithmetic  1.39 us (2%)
  between operations  1.3 us (2%)
    pallas_call x1, Pallas kernels, fused(): pl.pallas_call(functools.partial(fused_kernel, rcap, ccap), out_shape=[ja...  74 us
    unnamed x2, local copies, waits for them, and re-layouts  2 us

profile of v1, /device:TPU:0, one launch (start us, length us, event | category | flops | bytes accessed | tf_op | source)
XLA Modules:
  0.0 78.9 jit_solution(13638503999421826711)
XLA Ops:
  0.6 1.4 %shift-left_reduce_fusion = s32[]{:T(128)} fusion(s32[2,6]{1,0:T(2,128)} %param.11, s32[2]{0:T(128)S(1)} %iota_multiply_fusion), kind=kLoop, calls=%fused_computation.4 | loop fusion | flops 227 | bytes 60 | tf_op jit(solution)/shard_map/reduce_sum | solution.py:811
  2.7 74.2 %conditional.2 = ((f32[2,48,512]{2,1,0:T(8,128)S(1)}, f32[2,512,512]{2,1,0:T(8,128)S(1)})) conditional(s32[]{:T(128)} %convert_element_type.6, (s32[]{:T(128)}, f32[4096,2048]{1,0:T(8,128)}, f32[2,384,512]{2,1,0:T(8,128)}, s32[2,6]{1,0:T(2,128)}, f32[2,512,512]{2,1,0:T(8,128)}) %tuple.22, (f32[4096,2048]{1,0:T(8,128)}, f32[2,384,512]{2,1,0:T(8,128)}, ...), branch_computations={%region_1.4_spmd, %region_4.5_spmd} | conditional | flops 5 | bytes 106 | solution.py:824
  2.9 74.0 %branch_1_fun.3 = (f32[2,3,2,8,512]{4,3,2,1,0:T(8,128)S(1)}, f32[2,512,512]{2,1,0:T(8,128)S(1)}) custom-call(s32[2,6]{1,0:T(2,128)} %get-tuple-element.51.refs_0_, f32[16,256,2048]{2,1,0:T(8,128)} %bitcast.11, f32[2,24,2,8,512]{4,3,2,1,0:T(8,128)} %bitcast.14, f32[2,512,512]{2,1,0:T(8,128)} %get-tuple-element.54.refs_3_), custom_call_target="tpu_custom_call" | custom-call | tf_op jit(solution)/shard_map/cond/branch_1_fun/pallas_call | solution.py:788
  76.9 0.7 copy.20
  77.5 1.3 %copy.21 = f32[2,512,512]{2,1,0:T(8,128)} copy(f32[2,512,512]{2,1,0:T(8,128)S(1)} %get-tuple-element.74) | data formatting | bytes 4194304
  (1 shorter events, 0.0 us)
